TPU v7x, 256 devices: a whole 4x4x8 slice. The times are simulated.
256 devices in a mesh: seq: 64 (over z, x, core), head: 4 (over y).
Axes of the slice: x: 4, y: 4, z: 8, core: 2. Of those that a mesh axis runs over, the one named last changes fastest.
Arguments:
- query_key: bfloat16 [32768, 128], P('seq'), may hold values from -1.5 to 1.5
- values: bfloat16 [32768, 5120], P('seq', 'head'), may hold values from -0.119628906 to 0.119628906
- cotangent: bfloat16 [32768, 5120], P('seq', 'head'), may hold values from -0.119628906 to 0.119628906
- level_gain: float32 [16, 15, 80], P(None, None, 'head'), may hold values from 0.1 to 1
- level_code: int32 [512], P('seq'), may hold values from 0 to 15
Outputs:
- mixed: bfloat16 [32768, 5120], P('seq', 'head')
- grad_qk: float32 [32768, 128], P('seq')
- grad_values: bfloat16 [32768, 5120], P('seq', 'head')
Inputs may be any that keep to these rules, and one draw needn't show every extreme that they name: `level_code`: each span's row of the weight table.
All inputs are finite; a program needn't handle non-finite values.
Results may differ from a plain program's by a relative error of at most 0.005.
Values sent between devices are 32-bit elements; how exact they have to be, the bound alone decides.
No kernel may reach another device: no remote copies, remote signals or barrier semaphores. Data moves between devices by JAX's collectives and lax.ppermute only.
A program may use at most 128 MiB of HBM per device.

v0:
```python
import jax
import jax.numpy as jnp
from jax import lax
from jax.sharding import PartitionSpec as P

HEAD_DIM = 64
CH = 64
precise = lax.Precision.HIGHEST


def partner_2(value, axis, bit):
    mask = 2**bit
    pairs = [(source, source ^ mask) for source in range(lax.axis_size(axis))]
    return lax.ppermute(value, axis, pairs)


def bit_length(numbers, top_bits):
    bit_total = jnp.zeros_like(numbers)
    for bit_power in range(top_bits):
        bit_total = bit_total + (numbers >= 1 << bit_power).astype(jnp.int32)
    return bit_total


def local_levels(span_count):
    span_ids = jnp.arange(span_count, dtype=jnp.int32)
    return bit_length(span_ids[:, None] ^ span_ids[None, :], 8)


def local(query_key, values, cotangent, level_gain, level_code):
    tok_rows, state_dim = query_key.shape
    head_cols = values.shape[1]
    codes, levels, group_heads = level_gain.shape
    span_count = tok_rows // CH
    span_levels = span_count.bit_length() - 1
    seq_levels = lax.axis_size("seq").bit_length() - 1
    position = lax.axis_index("seq")
    picked = (level_code[:, None] == jnp.arange(codes, dtype=jnp.int32)[None, :]).astype(
        jnp.float32
    )
    level_weight = jnp.dot(
        picked, level_gain.reshape(codes, levels * group_heads), precision=precise
    ).reshape(span_count, levels, group_heads)
    cross_cols = jnp.repeat(
        level_weight[:, span_levels + 1 : span_levels + 1 + seq_levels, :], HEAD_DIM, axis=-1
    )
    own_state = lax.dot_general(
        query_key, values, (((0,), (0,)), ((), ())), preferred_element_type=jnp.float32
    )
    q_spans = query_key.reshape(span_count, CH, state_dim)
    c_spans = cotangent.reshape(span_count, CH, head_cols)
    span_grad = jnp.einsum("cti,ctj->cij", q_spans, c_spans, preferred_element_type=jnp.float32)
    level_grad = jnp.einsum("cij,clj->lij", span_grad, cross_cols, precision=precise)
    siblings = []
    adjoint = jnp.zeros_like(own_state)
    block_sum = own_state
    level_carry = level_grad
    for level_bit in range(seq_levels):
        partner = partner_2(block_sum, "seq", level_bit)
        upper_half = position >> level_bit & 1 == 1
        siblings.append(jnp.where(upper_half, partner, 0.0))
        block_sum = block_sum + partner
    for level_bit in range(seq_levels):
        partner_grad = partner_2(level_carry, "seq", level_bit)
        upper_half = position >> level_bit & 1 == 1
        adjoint = adjoint + jnp.where(upper_half, 0.0, partner_grad[0])
        level_carry = (level_carry + partner_grad)[1:]
    sibling = jnp.stack(siblings)
    span_state = jnp.einsum("clj,lij->cij", cross_cols, sibling, precision=precise).astype(
        jnp.bfloat16
    )
    adjoint_bf = adjoint.astype(jnp.bfloat16)
    scores = lax.dot_general(
        query_key, query_key, (((1,), (1,)), ((), ())), preferred_element_type=jnp.float32
    )
    onehot = (
        local_levels(span_count)[:, :, None]
        == jnp.arange(span_levels + 1, dtype=jnp.int32)[None, None, :]
    ).astype(jnp.float32)
    local_weight = jnp.einsum(
        "abk,akg->gab", onehot, level_weight[:, : span_levels + 1, :], precision=precise
    )
    causal = jnp.tril(jnp.ones((tok_rows, tok_rows), dtype=bool))
    pair_cols = 2 * HEAD_DIM

    def head_pair(pair_index, running):
        inner_out, dv_inner, d_score = running
        col_start = pair_index * pair_cols
        val_pair = lax.dynamic_slice_in_dim(values, col_start, pair_cols, 1).reshape(
            tok_rows, 2, HEAD_DIM
        )
        cot_pair = lax.dynamic_slice_in_dim(cotangent, col_start, pair_cols, 1).reshape(
            tok_rows, 2, HEAD_DIM
        )
        pair_weight = lax.dynamic_slice_in_dim(local_weight, pair_index * 2, 2, 0)
        weight = jnp.broadcast_to(
            pair_weight[:, :, None, :, None], (2, span_count, CH, span_count, CH)
        ).reshape(2, tok_rows, tok_rows)
        mixing = jnp.where(causal, weight * scores, 0.0).astype(jnp.bfloat16)
        part_out = jnp.einsum(
            "gts,sgp->tgp", mixing, val_pair, preferred_element_type=jnp.float32
        ).reshape(tok_rows, pair_cols)
        d_mix = jnp.einsum("tgp,sgp->gts", cot_pair, val_pair, preferred_element_type=jnp.float32)
        d_score = d_score + jnp.sum(jnp.where(causal, weight * d_mix, 0.0), axis=0)
        part_dv = jnp.einsum(
            "gts,tgp->sgp", mixing, cot_pair, preferred_element_type=jnp.float32
        ).reshape(tok_rows, pair_cols)
        inner_out = lax.dynamic_update_slice_in_dim(inner_out, part_out, col_start, 1)
        dv_inner = lax.dynamic_update_slice_in_dim(dv_inner, part_dv, col_start, 1)
        return (inner_out, dv_inner, d_score)

    start_state = (
        jnp.zeros((tok_rows, head_cols), jnp.float32),
        jnp.zeros((tok_rows, head_cols), jnp.float32),
        jnp.zeros((tok_rows, tok_rows), jnp.float32),
    )
    inner_out, dv_inner, d_score = lax.fori_loop(0, group_heads // 2, head_pair, start_state)
    outer_out = jnp.einsum(
        "cti,cij->ctj", q_spans, span_state, preferred_element_type=jnp.float32
    ).reshape(tok_rows, head_cols)
    mixed = (inner_out + outer_out).astype(jnp.bfloat16)
    dq_outer = jnp.einsum(
        "ctj,cij->cti", c_spans, span_state, preferred_element_type=jnp.float32
    ).reshape(tok_rows, state_dim)
    dv_outer = jnp.dot(query_key, adjoint_bf, preferred_element_type=jnp.float32)
    dk_outer = lax.dot_general(
        values, adjoint_bf, (((1,), (1,)), ((), ())), preferred_element_type=jnp.float32
    )
    q_float = query_key.astype(jnp.float32)
    dq_inner = jnp.dot(d_score, q_float, precision=precise) + lax.dot_general(
        d_score, q_float, (((0,), (0,)), ((), ())), precision=precise
    )
    head_part = dq_inner + dq_outer + dk_outer
    grad_qk = lax.psum(head_part, "head")
    grad_values = (dv_inner + dv_outer).astype(jnp.bfloat16)
    return (mixed, grad_qk, grad_values)


def solution(mesh):
    placed = (P("seq", None), P("seq", "head"), P("seq", "head"), P(None, None, "head"), P("seq"))
    return jax.shard_map(
        local,
        mesh=mesh,
        in_specs=placed,
        out_specs=(P("seq", "head"), P("seq", None), P("seq", "head")),
        check_vma=False,
    )
```

profile of v0, /device:TPU:2, one launch (start us, length us, event | category | flops | bytes accessed | tf_op | source)
XLA Modules:
  0.0 713.1 jit_solution(9387156875039487626)
XLA Ops:
  8.1 4.5 fusion.36
  12.6 6.3 copy.78
  19.9 2.7 copy-done.2
  24.0 10.4 %fusion.37 = f32[1280,6,128]{2,1,0:T(8,128)} fusion(f32[8,6,1280]{0,1,2:T(8,128)S(1)} %bitcast.108, f32[8,128,1280]{1,0,2:T(8,128)S(1)} %copy-done.4), kind=kOutput, calls=%fused_computation.70 | convolution fusion | flops 94371840 | bytes 9420800 | tf_op jit(solution)/shard_map/cij,clj->lij/dot_general | solution.py:52
  34.4 5.7 copy.79
  40.0 7.0 collective-permute-done.6
  47.0 3.8 slice_add_fusion
  53.2 71.2 %collective-permute-done.7 = f32[5,128,1280]{2,1,0:T(8,128)S(1)} collective-permute-done((f32[5,128,1280]{2,1,0:T(8,128)S(1)}, f32[5,128,1280]{2,1,0:T(8,128)S(1)}, u32[]{:S(2)}, u32[]{:S(2)}) %collective-permute-start.7) | collective-permute-done | bytes 3276832 | tf_op jit(solution)/shard_map/ppermute | solution.py:14
  135.8 64.5 %collective-permute-done.1 = f32[128,1280]{1,0:T(8,128)S(1)} collective-permute-done((f32[128,1280]{1,0:T(8,128)S(1)}, f32[128,1280]{1,0:T(8,128)S(1)}, u32[]{:S(2)}, u32[]{:S(2)}) %collective-permute-start.1) | collective-permute-done | bytes 655392 | tf_op jit(solution)/shard_map/ppermute | solution.py:14
  202.9 3.7 slice_add_fusion.2
  210.4 230.9 %while.19 = (s32[]{:T(128)}, f32[512,1280]{1,0:T(8,128)}, f32[512,1280]{0,1:T(8,128)}, f32[512,512]{1,0:T(8,128)}, bf16[512,1280]{1,0:T(8,128)(2,1)S(1)}, /*inde...) while((s32[]{:T(128)}, f32[512,1280]{1,0:T(8,128)}, ...), condition=%wide.region_2.3_spmd.clone.clone, body=%wide.region_0.2_spmd.clone.clone.sunk | while | flops 204996608 | bytes 29099832 | solution.py:116
  215.8 3.4 reshape.141
  238.0 3.4 reshape.141
  253.3 2.5 select_add_fusion.2
  258.8 2.4 broadcast_in_dim.103
  261.2 3.4 reshape.141
  276.4 2.5 select_add_fusion.2
  282.0 2.4 broadcast_in_dim.103
  284.4 3.4 reshape.141
  299.6 2.5 select_add_fusion.2
  305.2 2.4 broadcast_in_dim.103
  307.6 3.4 reshape.141
  322.8 2.5 select_add_fusion.2
  328.4 2.4 broadcast_in_dim.103
  330.8 3.4 reshape.141
  346.0 2.5 select_add_fusion.2
  351.6 2.4 broadcast_in_dim.103
  354.0 3.4 reshape.141
  369.2 2.5 select_add_fusion.2
  374.7 2.4 broadcast_in_dim.103
  377.1 3.4 reshape.141
  392.3 2.5 select_add_fusion.2
  400.3 3.4 reshape.141
  415.5 2.5 select_add_fusion.2
  421.1 2.4 broadcast_in_dim.103
  423.5 3.4 reshape.141
  438.7 2.5 select_add_fusion.2
  450.9 21.2 %collective-permute-done.3 = f32[128,1280]{1,0:T(8,128)S(1)} collective-permute-done((f32[128,1280]{1,0:T(8,128)S(1)}, f32[128,1280]{1,0:T(8,128)S(1)}, u32[]{:S(2)}, u32[]{:S(2)}) %collective-permute-start.3) | collective-permute-done | bytes 655392 | tf_op jit(solution)/shard_map/ppermute | solution.py:14
  474.1 59.5 %collective-permute-done.4 = f32[128,1280]{1,0:T(8,128)S(1)} collective-permute-done((f32[128,1280]{1,0:T(8,128)S(1)}, f32[128,1280]{1,0:T(8,128)S(1)}, u32[]{:S(2)}, u32[]{:S(2)}) %collective-permute-start.4) | collective-permute-done | bytes 655392 | tf_op jit(solution)/shard_map/ppermute | solution.py:14
  533.7 6.0 collective-permute-start.5
  541.9 34.5 %collective-permute-done.5 = f32[128,1280]{1,0:T(8,128)S(1)} collective-permute-done((f32[128,1280]{1,0:T(8,128)S(1)}, f32[128,1280]{1,0:T(8,128)S(1)}, u32[]{:S(2)}, u32[]{:S(2)}) %collective-permute-start.5) | collective-permute-done | bytes 655392 | tf_op jit(solution)/shard_map/ppermute | solution.py:14
  576.5 17.7 %collective-permute-done.11 = f32[1,128,1280]{2,1,0:T(8,128)S(1)} collective-permute-done((f32[1,128,1280]{2,1,0:T(8,128)S(1)}, f32[1,128,1280]{2,1,0:T(8,128)S(1)}, u32[]{:S(2)}, u32[]{:S(2)}) %collective-permute-start.11) | collective-permute-done | bytes 655392 | tf_op jit(solution)/shard_map/ppermute | solution.py:14
  594.2 3.0 fusion.9
  597.2 5.7 copy.73
  602.9 13.7 %convert_bitcast_fusion = bf16[8,128,1280]{1,0,2:T(8,128)(2,1)} fusion(f32[6,128,1280]{1,0,2:T(8,128)} %copy.73, f32[8,6,1280]{0,1,2:T(8,128)} %bitcast.109), kind=kOutput, calls=%fused_computation.17 | convolution fusion | flops 95682560 | bytes 6799360 | tf_op jit(solution)/shard_map/clj,lij->cij/dot_general | solution.py:68
  616.6 3.8 copy.75
  627.0 3.2 fusion.4
  632.3 72.3 %all-reduce.2.cloned.1.call-done = f32[512,128]{1,0:T(8,128)} async-done(((f32[512,128]{1,0:T(8,128)}), f32[512,128]{1,0:T(8,128)}) %all-reduce.2.cloned.1.call-update) | async-done | bytes 262160 | tf_op jit(solution)/shard_map/psum | solution.py:133
  (250 shorter events, 203.9 us)
Async XLA Ops:
  7.2 0.9 copy-start
  7.2 697.4 %all-reduce.2.cloned.1.call-start = ((), (), s32[]{:S(2)}) async-start(), calls=%async_computation | async-start | bytes 524288 | tf_op jit(solution)/shard_map/psum | solution.py:133
  12.6 6.3 copy-start.16
  12.6 6.6 copy-start.17
  19.6 4.4 copy-start.4
  19.9 2.7 copy-start.2
  40.0 7.0 collective-permute-start.6
  47.0 3.8 copy-start.10
  50.8 77.7 %copy-start.7 = (bf16[512,1280]{1,0:T(8,128)(2,1)S(1)}, bf16[512,1280]{1,0:T(8,128)(2,1)}, u32[]{:S(2)}) copy-start(bf16[512,1280]{1,0:T(8,128)(2,1)} %param.8) | copy-start | bytes 3932164
  50.8 73.6 %collective-permute-start.7 = (f32[5,128,1280]{2,1,0:T(8,128)S(1)}, f32[5,128,1280]{2,1,0:T(8,128)S(1)}, u32[]{:S(2)}, u32[]{:S(2)}) collective-permute-start(f32[5,128,1280]{2,1,0:T(8,128)S(1)} %slice_add_fusion), channel_id=1, source_target_pairs={{0,8},{4,12},{8,0},{12,4},{16,24},{20,28},{24,16},{28,20},{32,40},... | collective-permute-start | bytes 9830408 | tf_op jit(solution)/shard_map/ppermute | solution.py:14
  124.4 2.5 copy-start.11
  126.9 76.0 %collective-permute-start.8 = (f32[4,128,1280]{2,1,0:T(8,128)}, f32[4,128,1280]{2,1,0:T(8,128)}, u32[]{:S(2)}, u32[]{:S(2)}) collective-permute-start(f32[4,128,1280]{2,1,0:T(8,128)} %slice_add_fusion.1), channel_id=1, source_target_pairs={{0,16},{4,20},{8,24},{12,28},{16,0},{20,4},{24,8},{28,12},{32,48},... | collective-permute-start | bytes 7864328 | tf_op jit(solution)/shard_map/ppermute | solution.py:14
  128.9 2.2 collective-permute-start
  132.0 68.3 %collective-permute-start.1 = (f32[128,1280]{1,0:T(8,128)S(1)}, f32[128,1280]{1,0:T(8,128)S(1)}, u32[]{:S(2)}, u32[]{:S(2)}) collective-permute-start(f32[128,1280]{1,0:T(8,128)S(1)} %add.163), channel_id=1, source_target_pairs={{0,8},{4,12},{8,0},{12,4},{16,24},{20,28},{24,16},{28,20},{32,40},... | collective-permute-start | bytes 1966088 | tf_op jit(solution)/shard_map/ppermute | solution.py:14
  200.2 6.3 copy-start.12
  201.3 241.8 %collective-permute-start.2 = (f32[128,1280]{1,0:T(8,128)}, f32[128,1280]{1,0:T(8,128)}, u32[]{:S(2)}, u32[]{:S(2)}) collective-permute-start(f32[128,1280]{1,0:T(8,128)} %add.164), channel_id=1, source_target_pairs={{0,16},{4,20},{8,24},{12,28},{16,0},{20,4},{24,8},{28,12},{32,48},... | collective-permute-start | bytes 1966088 | tf_op jit(solution)/shard_map/ppermute | solution.py:14
  206.6 239.8 %collective-permute-start.9 = (f32[3,128,1280]{2,1,0:T(8,128)}, f32[3,128,1280]{2,1,0:T(8,128)}, u32[]{:S(2)}, u32[]{:S(2)}) collective-permute-start(f32[3,128,1280]{2,1,0:T(8,128)} %slice_add_fusion.2), channel_id=1, source_target_pairs={{0,32},{4,36},{8,40},{12,44},{16,48},{20,52},{24,56},{28,60},{32,0... | collective-permute-start | bytes 5898248 | tf_op jit(solution)/shard_map/ppermute | solution.py:14
  219.2 1.8 copy-start.3
  231.0 1.6 copy-start.8
  241.5 1.8 copy-start.3
  253.3 2.5 copy-start.8
  264.7 1.8 copy-start.3
  276.4 2.5 copy-start.8
  287.8 1.8 copy-start.3
  299.6 2.5 copy-start.8
  311.0 1.8 copy-start.3
  322.8 2.5 copy-start.8
  334.2 1.8 copy-start.3
  346.0 2.5 copy-start.8
  357.4 1.8 copy-start.3
  369.2 2.5 copy-start.8
  380.6 1.8 copy-start.3
  392.3 2.5 copy-start.8
  403.8 1.8 copy-start.3
  415.5 2.5 copy-start.8
  426.9 1.8 copy-start.3
  438.7 2.5 copy-start.8
  443.1 6.9 copy-start.15
  444.5 27.6 %collective-permute-start.3 = (f32[128,1280]{1,0:T(8,128)S(1)}, f32[128,1280]{1,0:T(8,128)S(1)}, u32[]{:S(2)}, u32[]{:S(2)}) collective-permute-start(f32[128,1280]{1,0:T(8,128)S(1)} %add.165), channel_id=1, source_target_pairs={{0,32},{4,36},{8,40},{12,44},{16,48},{20,52},{24,56},{28,60},{32,0... | collective-permute-start | bytes 1966088 | tf_op jit(solution)/shard_map/ppermute | solution.py:14
  448.2 24.1 %copy-start.13 = (f32[128,1280]{1,0:T(8,128)S(1)}, f32[128,1280]{1,0:T(8,128)}, u32[]{:S(2)}) copy-start(f32[128,1280]{1,0:T(8,128)} %copy-done.12) | copy-start | bytes 1966084
  448.2 91.6 %collective-permute-start.10 = (f32[2,128,1280]{2,1,0:T(8,128)S(1)}, f32[2,128,1280]{2,1,0:T(8,128)S(1)}, u32[]{:S(2)}, u32[]{:S(2)}) collective-permute-start(f32[2,128,1280]{2,1,0:T(8,128)S(1)} %slice_add_fusion.3), channel_id=1, source_target_pairs={{0,64},{4,68},{8,72},{12,76},{16,80},{20,84},{24,88},{28,92},{32,9... | collective-permute-start | bytes 3932168 | tf_op jit(solution)/shard_map/ppermute | solution.py:14
  472.2 61.5 %collective-permute-start.4 = (f32[128,1280]{1,0:T(8,128)S(1)}, f32[128,1280]{1,0:T(8,128)S(1)}, u32[]{:S(2)}, u32[]{:S(2)}) collective-permute-start(f32[128,1280]{1,0:T(8,128)S(1)} %add.166), channel_id=1, source_target_pairs={{0,64},{4,68},{8,72},{12,76},{16,80},{20,84},{24,88},{28,92},{32,9... | collective-permute-start | bytes 1966088 | tf_op jit(solution)/shard_map/ppermute | solution.py:14
  533.7 42.7 %collective-permute-start.5 = (f32[128,1280]{1,0:T(8,128)S(1)}, f32[128,1280]{1,0:T(8,128)S(1)}, u32[]{:S(2)}, u32[]{:S(2)}) collective-permute-start(f32[128,1280]{1,0:T(8,128)S(1)} %add.167), channel_id=1, source_target_pairs={{0,128},{4,132},{8,136},{12,140},{16,144},{20,148},{24,152},{28,15... | collective-permute-start | bytes 1966088 | tf_op jit(solution)/shard_map/ppermute | solution.py:14
  539.9 54.4 %collective-permute-start.11 = (f32[1,128,1280]{2,1,0:T(8,128)S(1)}, f32[1,128,1280]{2,1,0:T(8,128)S(1)}, u32[]{:S(2)}, u32[]{:S(2)}) collective-permute-start(f32[1,128,1280]{2,1,0:T(8,128)S(1)} %slice_add_fusion.4), channel_id=1, source_target_pairs={{0,128},{4,132},{8,136},{12,140},{16,144},{20,148},{24,152},{28,15... | collective-permute-start | bytes 1966088 | tf_op jit(solution)/shard_map/ppermute | solution.py:14
  622.8 2.0 copy-start.1
  622.8 3.0 copy-start.9
  624.8 2.3 copy-start.5
  627.0 3.2 copy-start.6
  (1 other events, 0.9 us)
Sparse Core Ops, SparseCore 0:
  627.1 77.3 all-reduce.1
where the time goes:
time: 717 us; the launch traced here: 713 us
  waiting for transfers between devices  350 us (49%)
  local copies, waits for them, and re-layouts  184 us (26%)
  matrix products  80 us (11%)
  other arithmetic  66.8 us (9%)
  starting transfers between devices  17.5 us (2%)
  between operations  14.3 us (2%)
    ppermute x12, waiting for transfers between devices, partner_2(): return lax.ppermute(value, axis, pairs)  278 us
    psum x1, waiting for transfers between devices, local(): grad_qk = lax.psum(head_part, 'head')  72.3 us
    dynamic_update_slice x20, local copies, waits for them, and re-layouts, head_pair(): lax.dynamic_update_slice_in_dim(inner_out, part_out, col_start, 1)  35 us
    reshape x10, local copies, waits for them, and re-layouts, head_pair(): weight = jnp.broadcast_to(pair_weight[:, :, None, :, None], (2, span_coun...  34.2 us
    dynamic_slice x20, local copies, waits for them, and re-layouts, head_pair(): lax.dynamic_slice_in_dim(cotangent, col_start, pair_cols, 1)  32.4 us
    broadcast_in_dim x10, local copies, waits for them, and re-layouts, head_pair(): jnp.broadcast_to(pair_weight[:, :, None, :, None], (2, span_count, CH, sp...  24 us
    add x10, other arithmetic, head_pair(): d_score = d_score + jnp.sum(jnp.where(causal, weight * d_mix, 0.0), axis=0)  23.9 us
    ppermute x12, starting transfers between devices, partner_2(): return lax.ppermute(value, axis, pairs)  17.5 us
  transfers between devices with their start and end apart: 13, of which 9 were waited for; matrix products, arithmetic and copies ran while one was open for 36% of the time, Pallas kernels for 0%

commit v1 on v0

--- a/solution.py
+++ b/solution.py
@@ -130,7 +130,9 @@
         d_score, q_float, (((0,), (0,)), ((), ())), precision=precise
     )
     head_part = dq_inner + dq_outer + dk_outer
-    grad_qk = lax.psum(head_part, "head")
+    grad_qk = head_part
+    for hop in (1, 2):
+        grad_qk = grad_qk + lax.ppermute(grad_qk, "head", [(dev, dev ^ hop) for dev in range(4)])
     grad_values = (dv_inner + dv_outer).astype(jnp.bfloat16)
     return (mixed, grad_qk, grad_values)
 

time: 717 us -> 669 us (0.933)
  the two profiles are of different devices: /device:TPU:2 before, /device:TPU:120 now
where the time goes in v1:
time: 669 us; the launch traced here: 665 us
  waiting for transfers between devices  261 us (39%)
  local copies, waits for them, and re-layouts  183 us (27%)
  matrix products  77.7 us (12%)
  starting transfers between devices  76.7 us (11%)
  other arithmetic  65.8 us (10%)
    ppermute x12, waiting for transfers between devices, partner_2(): return lax.ppermute(value, axis, pairs)  252 us
    ppermute x12, starting transfers between devices, partner_2(): return lax.ppermute(value, axis, pairs)  74.6 us
    dynamic_update_slice x20, local copies, waits for them, and re-layouts, head_pair(): lax.dynamic_update_slice_in_dim(inner_out, part_out, col_start, 1)  35.1 us
    reshape x10, local copies, waits for them, and re-layouts, head_pair(): weight = jnp.broadcast_to(pair_weight[:, :, None, :, None], (2, span_coun...  34.2 us
    dynamic_slice x20, local copies, waits for them, and re-layouts, head_pair(): lax.dynamic_slice_in_dim(cotangent, col_start, pair_cols, 1)  32.4 us
    add x10, other arithmetic, head_pair(): d_score = d_score + jnp.sum(jnp.where(causal, weight * d_mix, 0.0), axis=0)  23.9 us
    broadcast_in_dim x10, local copies, waits for them, and re-layouts, head_pair(): jnp.broadcast_to(pair_weight[:, :, None, :, None], (2, span_count, CH, sp...  23.9 us
    dot_general x10, matrix products, head_pair(): jnp.einsum('tgp,sgp->gts', cot_pair, val_pair, preferred_element_type=jnp...  17 us
  transfers between devices with their start and end apart: 14, of which 10 were waited for; matrix products, arithmetic and copies ran while one was open for 38% of the time, Pallas kernels for 0%

profile of v1, /device:TPU:120, one launch (start us, length us, event | category | flops | bytes accessed | tf_op | source)
XLA Modules:
  0.0 665.3 jit_solution(14044279545544186264)
XLA Ops:
  1.5 4.5 fusion.36
  6.1 6.3 copy.78
  13.4 2.7 copy-done.2
  17.4 10.3 %fusion.37 = f32[1280,6,128]{2,1,0:T(8,128)} fusion(f32[8,6,1280]{0,1,2:T(8,128)S(1)} %bitcast.108, f32[8,128,1280]{1,0,2:T(8,128)S(1)} %copy-done.4), kind=kOutput, calls=%fused_computation.70 | convolution fusion | flops 94371840 | bytes 9420800 | tf_op jit(solution)/shard_map/cij,clj->lij/dot_general | solution.py:52
  27.7 5.7 copy.79
  33.4 7.0 %collective-permute-done.6 = f32[6,128,1280]{2,1,0:T(8,128)S(1)} collective-permute-done((f32[6,128,1280]{2,1,0:T(8,128)}, f32[6,128,1280]{2,1,0:T(8,128)S(1)}, u32[]{:S(2)}, u32[]{:S(2)}) %collective-permute-start.6) | collective-permute-done | bytes 3932192 | tf_op jit(solution)/shard_map/ppermute | solution.py:14
  40.4 3.8 slice_add_fusion
  45.8 71.5 %collective-permute-done.7 = f32[5,128,1280]{2,1,0:T(8,128)S(1)} collective-permute-done((f32[5,128,1280]{2,1,0:T(8,128)S(1)}, f32[5,128,1280]{2,1,0:T(8,128)S(1)}, u32[]{:S(2)}, u32[]{:S(2)}) %collective-permute-start.7) | collective-permute-done | bytes 3276832 | tf_op jit(solution)/shard_map/ppermute | solution.py:14
  119.8 3.0 collective-permute-start.8
  129.2 64.5 %collective-permute-done.1 = f32[128,1280]{1,0:T(8,128)S(1)} collective-permute-done((f32[128,1280]{1,0:T(8,128)S(1)}, f32[128,1280]{1,0:T(8,128)S(1)}, u32[]{:S(2)}, u32[]{:S(2)}) %collective-permute-start.1) | collective-permute-done | bytes 655392 | tf_op jit(solution)/shard_map/ppermute | solution.py:14
  196.8 3.7 slice_add_fusion.2
  204.1 231.0 %while.19 = (s32[]{:T(128)}, f32[512,1280]{1,0:T(8,128)}, f32[512,1280]{0,1:T(8,128)}, f32[512,512]{1,0:T(8,128)}, bf16[512,1280]{1,0:T(8,128)(2,1)S(1)}, /*inde...) while((s32[]{:T(128)}, f32[512,1280]{1,0:T(8,128)}, ...), condition=%wide.region_2.3_spmd.clone.clone, body=%wide.region_0.2_spmd.clone.clone.sunk | while | flops 204996608 | bytes 29099832 | solution.py:116
  207.1 2.4 broadcast_in_dim.103
  209.5 3.4 reshape.141
  229.4 2.4 broadcast_in_dim.103
  231.8 3.4 reshape.141
  247.0 2.5 select_add_fusion.2
  252.6 2.4 broadcast_in_dim.103
  255.0 3.4 reshape.141
  270.2 2.5 select_add_fusion.2
  275.8 2.4 broadcast_in_dim.103
  278.2 3.4 reshape.141
  293.4 2.5 select_add_fusion.2
  301.4 3.4 reshape.141
  316.6 2.5 select_add_fusion.2
  322.2 2.4 broadcast_in_dim.103
  324.6 3.4 reshape.141
  339.8 2.5 select_add_fusion.2
  347.7 3.4 reshape.141
  362.9 2.5 select_add_fusion.2
  370.9 3.4 reshape.141
  386.2 2.5 select_add_fusion.2
  394.1 3.4 reshape.141
  409.3 2.5 select_add_fusion.2
  417.3 3.4 reshape.141
  432.5 2.5 select_add_fusion.2
  443.2 18.7 %collective-permute-done.3 = f32[128,1280]{1,0:T(8,128)S(1)} collective-permute-done((f32[128,1280]{1,0:T(8,128)S(1)}, f32[128,1280]{1,0:T(8,128)S(1)}, u32[]{:S(2)}, u32[]{:S(2)}) %collective-permute-start.3) | collective-permute-done | bytes 655392 | tf_op jit(solution)/shard_map/ppermute | solution.py:14
  462.0 3.4 collective-permute-start.4
  467.2 60.4 %collective-permute-done.4 = f32[128,1280]{1,0:T(8,128)S(1)} collective-permute-done((f32[128,1280]{1,0:T(8,128)S(1)}, f32[128,1280]{1,0:T(8,128)S(1)}, u32[]{:S(2)}, u32[]{:S(2)}) %collective-permute-start.4) | collective-permute-done | bytes 655392 | tf_op jit(solution)/shard_map/ppermute | solution.py:14
  527.7 61.3 %collective-permute-start.5 = (f32[128,1280]{1,0:T(8,128)S(1)}, f32[128,1280]{1,0:T(8,128)S(1)}, u32[]{:S(2)}, u32[]{:S(2)}) collective-permute-start(f32[128,1280]{1,0:T(8,128)S(1)} %add.171), channel_id=1, source_target_pairs={{0,128},{4,132},{8,136},{12,140},{16,144},{20,148},{24,152},{28,15... | collective-permute-start | bytes 1966088 | tf_op jit(solution)/shard_map/ppermute | solution.py:14
  591.1 13.0 %collective-permute-done.5 = f32[128,1280]{1,0:T(8,128)S(1)} collective-permute-done((f32[128,1280]{1,0:T(8,128)S(1)}, f32[128,1280]{1,0:T(8,128)S(1)}, u32[]{:S(2)}, u32[]{:S(2)}) %collective-permute-start.5) | collective-permute-done | bytes 655392 | tf_op jit(solution)/shard_map/ppermute | solution.py:14
  604.2 14.6 %collective-permute-done.11 = f32[1,128,1280]{2,1,0:T(8,128)S(1)} collective-permute-done((f32[1,128,1280]{2,1,0:T(8,128)S(1)}, f32[1,128,1280]{2,1,0:T(8,128)S(1)}, u32[]{:S(2)}, u32[]{:S(2)}) %collective-permute-start.11) | collective-permute-done | bytes 655392 | tf_op jit(solution)/shard_map/ppermute | solution.py:14
  618.8 3.0 fusion.9
  621.8 5.8 copy.73
  627.5 13.7 %convert_bitcast_fusion = bf16[8,128,1280]{1,0,2:T(8,128)(2,1)} fusion(f32[6,128,1280]{1,0,2:T(8,128)} %copy.73, f32[8,6,1280]{0,1,2:T(8,128)} %bitcast.109), kind=kOutput, calls=%fused_computation.17 | convolution fusion | flops 95682560 | bytes 6799360 | tf_op jit(solution)/shard_map/clj,lij->cij/dot_general | solution.py:68
  641.2 3.8 copy.75
  652.4 4.2 collective-permute-done.12
  659.9 4.7 collective-permute-done.13
  (252 shorter events, 205.5 us)
Async XLA Ops:
  6.1 6.3 copy-start.16
  6.1 6.6 copy-start.17
  13.0 4.4 copy-start.4
  13.4 2.7 copy-start.2
  33.4 7.0 %collective-permute-start.6 = (f32[6,128,1280]{2,1,0:T(8,128)}, f32[6,128,1280]{2,1,0:T(8,128)S(1)}, u32[]{:S(2)}, u32[]{:S(2)}) collective-permute-start(f32[6,128,1280]{2,1,0:T(8,128)} %bitcast.116), channel_id=1, source_target_pairs={{0,4},{4,0},{8,12},{12,8},{16,20},{20,16},{24,28},{28,24},{32,36},... | collective-permute-start | bytes 11796488 | tf_op jit(solution)/shard_map/ppermute | solution.py:14
  40.4 3.8 copy-start.10
  44.2 78.6 %copy-start.7 = (bf16[512,1280]{1,0:T(8,128)(2,1)S(1)}, bf16[512,1280]{1,0:T(8,128)(2,1)}, u32[]{:S(2)}) copy-start(bf16[512,1280]{1,0:T(8,128)(2,1)} %param.8) | copy-start | bytes 3932164
  44.2 73.0 %collective-permute-start.7 = (f32[5,128,1280]{2,1,0:T(8,128)S(1)}, f32[5,128,1280]{2,1,0:T(8,128)S(1)}, u32[]{:S(2)}, u32[]{:S(2)}) collective-permute-start(f32[5,128,1280]{2,1,0:T(8,128)S(1)} %slice_add_fusion), channel_id=1, source_target_pairs={{0,8},{4,12},{8,0},{12,4},{16,24},{20,28},{24,16},{28,20},{32,40},... | collective-permute-start | bytes 9830408 | tf_op jit(solution)/shard_map/ppermute | solution.py:14
  117.2 2.6 copy-start.11
  119.8 77.0 %collective-permute-start.8 = (f32[4,128,1280]{2,1,0:T(8,128)}, f32[4,128,1280]{2,1,0:T(8,128)}, u32[]{:S(2)}, u32[]{:S(2)}) collective-permute-start(f32[4,128,1280]{2,1,0:T(8,128)} %slice_add_fusion.1), channel_id=1, source_target_pairs={{0,16},{4,20},{8,24},{12,28},{16,0},{20,4},{24,8},{28,12},{32,48},... | collective-permute-start | bytes 7864328 | tf_op jit(solution)/shard_map/ppermute | solution.py:14
  123.2 2.2 collective-permute-start
  126.3 67.4 %collective-permute-start.1 = (f32[128,1280]{1,0:T(8,128)S(1)}, f32[128,1280]{1,0:T(8,128)S(1)}, u32[]{:S(2)}, u32[]{:S(2)}) collective-permute-start(f32[128,1280]{1,0:T(8,128)S(1)} %add.167), channel_id=1, source_target_pairs={{0,8},{4,12},{8,0},{12,4},{16,24},{20,28},{24,16},{28,20},{32,40},... | collective-permute-start | bytes 1966088 | tf_op jit(solution)/shard_map/ppermute | solution.py:14
  193.7 6.8 %copy-start.12 = (f32[128,1280]{1,0:T(8,128)}, f32[128,1280]{1,0:T(8,128)S(1)}, u32[]{:S(2)}) copy-start(f32[128,1280]{1,0:T(8,128)S(1)} %collective-permute-done.1) | copy-start | bytes 1966084
  194.8 242.1 %collective-permute-start.2 = (f32[128,1280]{1,0:T(8,128)}, f32[128,1280]{1,0:T(8,128)}, u32[]{:S(2)}, u32[]{:S(2)}) collective-permute-start(f32[128,1280]{1,0:T(8,128)} %add.168), channel_id=1, source_target_pairs={{0,16},{4,20},{8,24},{12,28},{16,0},{20,4},{24,8},{28,12},{32,48},... | collective-permute-start | bytes 1966088 | tf_op jit(solution)/shard_map/ppermute | solution.py:14
  200.5 239.8 %collective-permute-start.9 = (f32[3,128,1280]{2,1,0:T(8,128)}, f32[3,128,1280]{2,1,0:T(8,128)}, u32[]{:S(2)}, u32[]{:S(2)}) collective-permute-start(f32[3,128,1280]{2,1,0:T(8,128)} %slice_add_fusion.2), channel_id=1, source_target_pairs={{0,32},{4,36},{8,40},{12,44},{16,48},{20,52},{24,56},{28,60},{32,0... | collective-permute-start | bytes 5898248 | tf_op jit(solution)/shard_map/ppermute | solution.py:14
  212.9 1.8 copy-start.3
  224.7 1.6 copy-start.8
  235.2 1.8 copy-start.3
  247.0 2.5 copy-start.8
  258.5 1.8 copy-start.3
  270.2 2.5 copy-start.8
  281.6 1.8 copy-start.3
  293.4 2.5 copy-start.8
  304.8 1.8 copy-start.3
  316.6 2.5 copy-start.8
  328.0 1.8 copy-start.3
  339.7 2.5 copy-start.8
  351.2 1.8 copy-start.3
  362.9 2.5 copy-start.8
  374.3 1.8 copy-start.3
  386.2 2.5 copy-start.8
  397.6 1.8 copy-start.3
  409.3 2.5 copy-start.8
  420.7 1.8 copy-start.3
  432.5 2.5 copy-start.8
  436.9 5.4 copy-start.15
  438.3 23.6 %collective-permute-start.3 = (f32[128,1280]{1,0:T(8,128)S(1)}, f32[128,1280]{1,0:T(8,128)S(1)}, u32[]{:S(2)}, u32[]{:S(2)}) collective-permute-start(f32[128,1280]{1,0:T(8,128)S(1)} %add.169), channel_id=1, source_target_pairs={{0,32},{4,36},{8,40},{12,44},{16,48},{20,52},{24,56},{28,60},{32,0... | collective-permute-start | bytes 1966088 | tf_op jit(solution)/shard_map/ppermute | solution.py:14
  442.2 23.2 %copy-start.13 = (f32[128,1280]{1,0:T(8,128)S(1)}, f32[128,1280]{1,0:T(8,128)}, u32[]{:S(2)}) copy-start(f32[128,1280]{1,0:T(8,128)} %copy-done.12) | copy-start | bytes 1966084
  442.2 146.8 %collective-permute-start.10 = (f32[2,128,1280]{2,1,0:T(8,128)S(1)}, f32[2,128,1280]{2,1,0:T(8,128)S(1)}, u32[]{:S(2)}, u32[]{:S(2)}) collective-permute-start(f32[2,128,1280]{2,1,0:T(8,128)S(1)} %slice_add_fusion.3), channel_id=1, source_target_pairs={{0,64},{4,68},{8,72},{12,76},{16,80},{20,84},{24,88},{28,92},{32,9... | collective-permute-start | bytes 3932168 | tf_op jit(solution)/shard_map/ppermute | solution.py:14
  462.0 65.6 %collective-permute-start.4 = (f32[128,1280]{1,0:T(8,128)S(1)}, f32[128,1280]{1,0:T(8,128)S(1)}, u32[]{:S(2)}, u32[]{:S(2)}) collective-permute-start(f32[128,1280]{1,0:T(8,128)S(1)} %add.170), channel_id=1, source_target_pairs={{0,64},{4,68},{8,72},{12,76},{16,80},{20,84},{24,88},{28,92},{32,9... | collective-permute-start | bytes 1966088 | tf_op jit(solution)/shard_map/ppermute | solution.py:14
  527.7 76.5 %collective-permute-start.5 = (f32[128,1280]{1,0:T(8,128)S(1)}, f32[128,1280]{1,0:T(8,128)S(1)}, u32[]{:S(2)}, u32[]{:S(2)}) collective-permute-start(f32[128,1280]{1,0:T(8,128)S(1)} %add.171), channel_id=1, source_target_pairs={{0,128},{4,132},{8,136},{12,140},{16,144},{20,148},{24,152},{28,15... | collective-permute-start | bytes 1966088 | tf_op jit(solution)/shard_map/ppermute | solution.py:14
  589.0 29.8 %collective-permute-start.11 = (f32[1,128,1280]{2,1,0:T(8,128)S(1)}, f32[1,128,1280]{2,1,0:T(8,128)S(1)}, u32[]{:S(2)}, u32[]{:S(2)}) collective-permute-start(f32[1,128,1280]{2,1,0:T(8,128)S(1)} %slice_add_fusion.4), channel_id=1, source_target_pairs={{0,128},{4,132},{8,136},{12,140},{16,144},{20,148},{24,152},{28,15... | collective-permute-start | bytes 1966088 | tf_op jit(solution)/shard_map/ppermute | solution.py:14
  647.4 1.2 copy-start.1
  647.4 2.2 copy-start.9
  647.9 3.0 copy-start.5
  650.1 6.5 collective-permute-start.12
  650.9 7.0 %copy-start.6 = (f32[512,1280]{0,1:T(8,128)S(1)}, f32[512,1280]{0,1:T(8,128)}, u32[]{:S(2)}) copy-start(f32[512,1280]{0,1:T(8,128)} %get-tuple-element.380) | copy-start | bytes 7864324
  656.6 8.0 %collective-permute-start.13 = (f32[512,128]{1,0:T(8,128)S(1)}, f32[512,128]{1,0:T(8,128)S(1)}, u32[]{:S(2)}, u32[]{:S(2)}) collective-permute-start(f32[512,128]{1,0:T(8,128)S(1)} %add.187), channel_id=1, source_target_pairs={{0,2},{1,3},{2,0},{3,1},{4,6},{5,7},{6,4},{7,5},{8,10},{9,11},{10,... | collective-permute-start | bytes 786440 | tf_op jit(solution)/shard_map/ppermute | solution.py:135
  (2 other events, 1.8 us)
